TPU v7x, 256 devices: a whole 4x4x8 slice. The times are simulated.
256 devices in a mesh: link: 32 (over z, x), intv: 8 (over y, core).
Axes of the slice: x: 4, y: 4, z: 8, core: 2. Of those that a mesh axis runs over, the one named last changes fastest.
Arguments:
- slab: bfloat16 [256, 16, 262144], P('intv', None, 'link'), may hold values from -6 to 6
- interval_factor: float32 [256, 64], P('intv'), may hold values from -6 to 6
- day_factor: float32 [16, 64], replicated, may hold values from -6 to 6
Outputs:
- link_new: float32 [262144, 64], P(('link', 'intv'))
- interval_new: float32 [256, 64], P('intv')
- day_new: float32 [16, 64], replicated
All inputs are finite; a program needn't handle non-finite values.
Results may differ from a plain program's by a relative error of at most 0.0024.
The roundings to bfloat16 on the way count: a program that leaves them out, or rounds other values in their place, can miss the bound.
Values may be sent and summed in bfloat16 or wider, within the bound.
No kernel may reach another device: no remote copies, remote signals or barrier semaphores. Data moves between devices by JAX's collectives and lax.ppermute only.
A program may use at most 64 MiB of HBM per device.

v0:
```python
import jax
import jax.numpy as jnp
from jax import lax
from jax.sharding import PartitionSpec as P


def solve_rows(system, rhs):
    rank = system.shape[0]
    shifted = system + 0.01 * jnp.trace(system) / rank * jnp.eye(rank, dtype=system.dtype)
    factor = jnp.linalg.cholesky(shifted)
    return jax.scipy.linalg.cho_solve((factor, True), rhs.T).T


def gram_of(matrix):
    return jnp.dot(matrix.T, matrix, precision=lax.Precision.HIGHEST)


def body(slab, interval_factor, day_factor):
    intervals, days, links = slab.shape
    rank = day_factor.shape[1]
    flat = slab.reshape(intervals * days, links)
    gram_day = gram_of(day_factor)
    gram_interval = lax.psum(gram_of(interval_factor), "intv")
    khatri = (
        (interval_factor[:, None, :] * day_factor[None, :, :])
        .reshape(intervals * days, rank)
        .astype(jnp.bfloat16)
    )
    system_link = gram_interval * gram_day
    owned_sums = lax.psum_scatter(
        lax.dot_general(flat, khatri, (((0,), (0,)), ((), ())), preferred_element_type=jnp.float32),
        "intv",
        scatter_dimension=0,
        tiled=True,
    )
    link_new = solve_rows(system_link, owned_sums)
    gram_link = lax.psum(gram_of(link_new), ("link", "intv"))
    link_block = lax.all_gather(link_new.astype(jnp.bfloat16), "intv", axis=0, tiled=True)
    partial_sums = jnp.dot(flat, link_block, preferred_element_type=jnp.float32).reshape(
        intervals, days, rank
    )
    interval_part = jnp.sum(partial_sums * day_factor[None, :, :], axis=1)
    interval_sums = lax.psum(interval_part, "link")
    interval_new = solve_rows(gram_link * gram_day, interval_sums)
    gram_new = lax.psum(gram_of(interval_new), "intv")
    day_part = jnp.sum(partial_sums * interval_new[:, None, :], axis=0)
    day_sums = lax.psum(day_part, ("link", "intv"))
    day_new = solve_rows(gram_link * gram_new, day_sums)
    return (link_new, interval_new, day_new)


def solution(mesh):
    placed = (P("intv", None, "link"), P("intv", None), P())
    return jax.shard_map(
        body,
        mesh=mesh,
        in_specs=placed,
        out_specs=(P(("link", "intv"), None), P("intv", None), P()),
        check_vma=False,
    )
```

profile of v0, /device:TPU:32, one launch (start us, length us, event | category | flops | bytes accessed | tf_op | source)
XLA Modules:
  0.0 413.3 jit_solution(11994552276993962413)
XLA Ops:
  7.2 6.4 %convolution_bitcast_fusion = f32[8192,64]{0,1:T(8,128)} fusion(bf16[32,16,8192]{2,1,0:T(8,128)(2,1)} %param.4, f32[16,64]{1,0:T(8,128)} %param.6, f32[32,64]{1,0:T(8,128)} %param.5), kind=kOutput, calls=%fused_computation | convolution fusion | flops 536936448 | bytes 10498048 | tf_op jit(solution)/shard_map/dot_general | solution.py:31
  13.9 25.9 %psum.35 = f32[64,64]{1,0:T(8,128)S(1)} all-reduce(f32[64,64]{1,0:T(8,128)S(1)} %fusion.32), channel_id=1, replica_groups=mesh['link'=32,'intv'=8] {'intv'}, use_global_device_ids=true, to_apply=%region_0.0 | all-reduce | flops 4096 | bytes 32768 | tf_op jit(solution)/shard_map/psum | solution.py:23
  39.8 0.8 fusion.26
  41.5 5.9 %cholesky.59 = f32[64,64]{1,0:T(8,128)S(1)} custom-call(f32[64,64]{1,0:T(8,128)S(1)} %copy.16), custom_call_target="Cholesky" | custom-call | tf_op jit(solution)/shard_map/jit(cholesky)/cholesky | solution.py:10
  47.4 0.6 compare_reduce_fusion.2
  48.1 0.7 fusion.2
  48.7 4.9 %custom-call.23 = f32[1,64,64]{1,2,0:T(8,128)S(1)} custom-call(f32[1,64,64]{2,1,0:T(8,128)S(1)} %fusion.2), custom_call_target="InvertDiagBlocksLowerTriangular" | custom-call | tf_op jit(solution)/shard_map/jit(_cho_solve)/triangular_solve | solution.py:11
  53.6 1.4 fusion.17
  55.4 0.7 bitcast_convert_fusion
  56.5 78.2 %psum.36 = f32[64,64]{1,0:T(8,128)S(1)} all-reduce(f32[64,64]{1,0:T(8,128)S(1)} %fusion.33), channel_id=1, replica_groups=mesh['link'=32,'intv'=8] {'link','intv'}, use_global_device_ids=true, to_apply=%region_5.7 | all-reduce | flops 4096 | bytes 32768 | tf_op jit(solution)/shard_map/psum | solution.py:37
  136.2 5.9 %cholesky.70 = f32[64,64]{1,0:T(8,128)S(1)} custom-call(f32[64,64]{1,0:T(8,128)S(1)} %copy.18), custom_call_target="Cholesky" | custom-call | tf_op jit(solution)/shard_map/jit(cholesky)/cholesky | solution.py:10
  142.1 0.6 compare_reduce_fusion.1
  142.7 0.7 fusion.3
  143.4 4.9 %custom-call.24 = f32[1,64,64]{1,2,0:T(8,128)S(1)} custom-call(f32[1,64,64]{2,1,0:T(8,128)S(1)} %fusion.3), custom_call_target="InvertDiagBlocksLowerTriangular" | custom-call | tf_op jit(solution)/shard_map/jit(_cho_solve)/triangular_solve | solution.py:11
  148.3 6.4 %convolution_bitcast_fusion.1 = f32[512,64]{0,1:T(8,128)S(1)} fusion(bf16[8192,64]{0,1:T(8,128)(2,1)} %all-gather.2.cloned.1.call-done, bf16[512,8192]{1,0:T(8,128)(2,1)} %bitcast.62), kind=kOutput, calls=%fused_computation.1 | convolution fusion | flops 536870912 | bytes 9568256 | tf_op jit(solution)/shard_map/dot_general | solution.py:39
  154.9 132.4 %psum.37 = f32[32,64]{1,0:T(8,128)S(1)} all-reduce(f32[32,64]{1,0:T(8,128)S(1)} %multiply_reduce_fusion.1), channel_id=1, replica_groups=mesh['link'=32,'intv'=8] {'link'}, use_global_device_ids=true, to_apply=%region_8.10 | all-reduce | flops 2048 | bytes 16384 | tf_op jit(solution)/shard_map/psum | solution.py:43
  288.1 80.1 %psum.39 = f32[16,64]{1,0:T(8,128)S(1)} all-reduce(f32[16,64]{1,0:T(8,128)S(1)} %multiply_reduce_fusion), channel_id=1, replica_groups=mesh['link'=32,'intv'=8] {'link','intv'}, use_global_device_ids=true, to_apply=%region_12.14 | all-reduce | flops 1024 | bytes 8192 | tf_op jit(solution)/shard_map/psum | solution.py:47
  368.2 23.6 %psum.38 = f32[64,64]{1,0:T(8,128)S(1)} all-reduce(f32[64,64]{1,0:T(8,128)S(1)} %fusion.34), channel_id=1, replica_groups=mesh['link'=32,'intv'=8] {'intv'}, use_global_device_ids=true, to_apply=%region_9.11 | all-reduce | flops 4096 | bytes 32768 | tf_op jit(solution)/shard_map/psum | solution.py:45
  391.8 0.6 fusion.30
  393.3 5.9 %cholesky.81 = f32[64,64]{1,0:T(8,128)S(1)} custom-call(f32[64,64]{1,0:T(8,128)S(1)} %copy.21), custom_call_target="Cholesky" | custom-call | tf_op jit(solution)/shard_map/jit(cholesky)/cholesky | solution.py:10
  399.2 0.6 compare_reduce_fusion
  399.8 0.7 fusion.4
  400.5 4.9 %custom-call.25 = f32[1,64,64]{1,2,0:T(8,128)S(1)} custom-call(f32[1,64,64]{2,1,0:T(8,128)S(1)} %fusion.4), custom_call_target="InvertDiagBlocksLowerTriangular" | custom-call | tf_op jit(solution)/shard_map/jit(_cho_solve)/triangular_solve | solution.py:11
  405.6 0.8 fusion.5
  (40 shorter events, 3.5 us)
Async XLA Ops:
  7.2 32.7 %copy-start.3 = (f32[16,64]{1,0:T(8,128)S(1)}, f32[16,64]{1,0:T(8,128)}, u32[]{:S(2)}) copy-start(f32[16,64]{1,0:T(8,128)} %param.6) | copy-start | bytes 12292
  7.2 6.5 %copy-start.1 = (f32[32,64]{1,0:T(8,128)S(1)}, f32[32,64]{1,0:T(8,128)}, u32[]{:S(2)}) copy-start(f32[32,64]{1,0:T(8,128)} %param.5) | copy-start | bytes 24580
  7.2 46.4 %reduce-scatter.2.cloned.1.call-start = ((), (), s32[]{:S(2)}) async-start(), calls=%async_computation.1 | async-start | bytes 2359296 | tf_op jit(solution)/shard_map/reduce_scatter | solution.py:30
  13.6 134.7 %all-gather.2.cloned.1.call-start = ((), (), s32[]{:S(2)}) async-start(), calls=%async_computation.2 | async-start | bytes 1179648 | tf_op jit(solution)/shard_map/all_gather | solution.py:38
  55.4 351.1 %copy-start = (f32[64,1024]{1,0:T(8,128)}, f32[64,1024]{1,0:T(8,128)S(1)}, u32[]{:S(2)}) copy-start(f32[64,1024]{1,0:T(8,128)S(1)} %fusion.15) | copy-start | bytes 786436
  287.8 118.7 %copy-start.2 = (f32[64,32]{0,1:T(8,128)}, f32[64,32]{0,1:T(8,128)S(1)}, u32[]{:S(2)}) copy-start(f32[64,32]{0,1:T(8,128)S(1)} %fusion.10) | copy-start | bytes 24580
Sparse Core Ops, SparseCore 0:
  13.8 38.8 reduce-scatter.1
  56.3 25.8 all-gather.1
where the time goes:
time: 414 us; the launch traced here: 413 us
  blocking collectives  340 us (82%)
  other arithmetic  38.4 us (9%)
  matrix products  17.7 us (4%)
  between operations  16.2 us (4%)
    psum x1, blocking collectives, body(): interval_sums = lax.psum(interval_part, 'link')  132 us
    psum x1, blocking collectives, body(): day_sums = lax.psum(day_part, ('link', 'intv'))  80.1 us
    psum x1, blocking collectives, body(): gram_link = lax.psum(gram_of(link_new), ('link', 'intv'))  78.2 us
    psum x1, blocking collectives, body(): gram_interval = lax.psum(gram_of(interval_factor), 'intv')  25.9 us
    psum x1, blocking collectives, body(): gram_new = lax.psum(gram_of(interval_new), 'intv')  23.6 us
    another operation x9, other arithmetic, solve_rows(): factor = jnp.linalg.cholesky(shifted)  19.6 us
    another operation x6, other arithmetic, solve_rows(): return jax.scipy.linalg.cho_solve((factor, True), rhs.T).T  16.6 us
  transfers between devices with their start and end apart: 2, of which 0 were waited for; matrix products, arithmetic and copies ran while one was open for 6% of the time, Pallas kernels for 0%

commit v1 on v0

--- a/solution.py
+++ b/solution.py
@@ -40,7 +40,11 @@
         intervals, days, rank
     )
     interval_part = jnp.sum(partial_sums * day_factor[None, :, :], axis=1)
-    interval_sums = lax.psum(interval_part, "link")
+    interval_sums = interval_part
+    for hop in (1, 2, 4, 8, 16):
+        interval_sums = interval_sums + lax.ppermute(
+            interval_sums, "link", [(dev, dev ^ hop) for dev in range(32)]
+        )
     interval_new = solve_rows(gram_link * gram_day, interval_sums)
     gram_new = lax.psum(gram_of(interval_new), "intv")
     day_part = jnp.sum(partial_sums * interval_new[:, None, :], axis=0)

time: 414 us -> 291 us (0.70)
  blocking collectives: 340 us -> 202 us
  waiting for transfers between devices: 0.09 us -> 9.7 us
  starting transfers between devices: 0.08 us -> 6.36 us
    psum x1 -> x0, blocking collectives: 132 us -> none  [body(): interval_sums = lax.psum(interval_part, 'link')]
    ppermute x0 -> x5, waiting for transfers between devices: none -> 9.62 us  [body(): lax.ppermute(interval_sums, 'link', [(dev, dev ^ hop) for dev in range(32)])]
    psum x1, blocking collectives: 80.1 us -> 72.9 us  [body(): day_sums = lax.psum(day_part, ('link', 'intv'))]
    ppermute x0 -> x5, starting transfers between devices: none -> 6.28 us  [body(): lax.ppermute(interval_sums, 'link', [(dev, dev ^ hop) for dev in range(32)])]
  transfers between devices with their start and end apart: 2 -> 7, of which waited for: 0 -> 3; matrix products, arithmetic and copies ran while one was open for 6% -> 9% of each run, Pallas kernels for 0% -> 0%
where the time goes in v1:
time: 291 us
  blocking collectives  202 us (69%)
  other arithmetic  38.4 us (13%)
  matrix products  17.7 us (6%)
  between operations  16.3 us (6%)
  waiting for transfers between devices  9.7 us (3%)
  starting transfers between devices  6.36 us (2%)
    psum x1, blocking collectives, body(): gram_link = lax.psum(gram_of(link_new), ('link', 'intv'))  78.3 us
    psum x1, blocking collectives, body(): day_sums = lax.psum(day_part, ('link', 'intv'))  72.9 us
    psum x1, blocking collectives, body(): gram_interval = lax.psum(gram_of(interval_factor), 'intv')  25.9 us
    psum x1, blocking collectives, body(): gram_new = lax.psum(gram_of(interval_new), 'intv')  24.6 us
    another operation x9, other arithmetic, solve_rows(): factor = jnp.linalg.cholesky(shifted)  19.6 us
    another operation x6, other arithmetic, solve_rows(): return jax.scipy.linalg.cho_solve((factor, True), rhs.T).T  16.6 us
    ppermute x5, waiting for transfers between devices, body(): lax.ppermute(interval_sums, 'link', [(dev, dev ^ hop) for dev in range(32)])  9.62 us
    dot_general x1, matrix products, body(): lax.dot_general(flat, khatri, (((0,), (0,)), ((), ())), preferred_element...  6.38 us
  transfers between devices with their start and end apart: 7, of which 3 were waited for; matrix products, arithmetic and copies ran while one was open for 9% of the time, Pallas kernels for 0%

profile of v1, /device:TPU:32, one launch (start us, length us, event | category | flops | bytes accessed | tf_op | source)
XLA Modules:
  0.0 290.6 jit_solution(6447470152435768004)
XLA Ops:
  7.2 6.4 %convolution_bitcast_fusion = f32[8192,64]{0,1:T(8,128)} fusion(bf16[32,16,8192]{2,1,0:T(8,128)(2,1)} %param.4, f32[16,64]{1,0:T(8,128)} %param.6, f32[32,64]{1,0:T(8,128)} %param.5), kind=kOutput, calls=%fused_computation | convolution fusion | flops 536936448 | bytes 10498048 | tf_op jit(solution)/shard_map/dot_general | solution.py:31
  13.9 25.9 %psum.28 = f32[64,64]{1,0:T(8,128)S(1)} all-reduce(f32[64,64]{1,0:T(8,128)S(1)} %fusion.33), channel_id=1, replica_groups=mesh['link'=32,'intv'=8] {'intv'}, use_global_device_ids=true, to_apply=%region_0.0 | all-reduce | flops 4096 | bytes 32768 | tf_op jit(solution)/shard_map/psum | solution.py:23
  39.8 0.8 fusion.26
  41.5 5.9 %cholesky.59 = f32[64,64]{1,0:T(8,128)S(1)} custom-call(f32[64,64]{1,0:T(8,128)S(1)} %copy.16), custom_call_target="Cholesky" | custom-call | tf_op jit(solution)/shard_map/jit(cholesky)/cholesky | solution.py:10
  48.1 0.7 fusion.2
  48.7 4.9 %custom-call.23 = f32[1,64,64]{1,2,0:T(8,128)S(1)} custom-call(f32[1,64,64]{2,1,0:T(8,128)S(1)} %fusion.2), custom_call_target="InvertDiagBlocksLowerTriangular" | custom-call | tf_op jit(solution)/shard_map/jit(_cho_solve)/triangular_solve | solution.py:11
  53.6 1.4 fusion.17
  55.4 0.7 bitcast_convert_fusion
  56.5 78.3 %psum.29 = f32[64,64]{1,0:T(8,128)S(1)} all-reduce(f32[64,64]{1,0:T(8,128)S(1)} %fusion.34), channel_id=1, replica_groups=mesh['link'=32,'intv'=8] {'link','intv'}, use_global_device_ids=true, to_apply=%region_5.7 | all-reduce | flops 4096 | bytes 32768 | tf_op jit(solution)/shard_map/psum | solution.py:37
  136.1 6.4 %convolution_bitcast_fusion.1 = f32[512,64]{0,1:T(8,128)S(1)} fusion(bf16[8192,64]{0,1:T(8,128)(2,1)} %all-gather.2.cloned.1.call-done, bf16[512,8192]{1,0:T(8,128)(2,1)} %bitcast.61), kind=kOutput, calls=%fused_computation.1 | convolution fusion | flops 536870912 | bytes 9568256 | tf_op jit(solution)/shard_map/dot_general | solution.py:39
  142.9 3.6 %collective-permute-done = f32[32,64]{1,0:T(8,128)S(1)} collective-permute-done((f32[32,64]{1,0:T(8,128)S(1)}, f32[32,64]{1,0:T(8,128)S(1)}, u32[]{:S(2)}, u32[]{:S(2)}) %collective-permute-start) | collective-permute-done | bytes 8224 | tf_op jit(solution)/shard_map/ppermute | solution.py:45
  146.5 1.2 collective-permute-start.1
  147.8 5.9 %cholesky.70 = f32[64,64]{1,0:T(8,128)S(1)} custom-call(f32[64,64]{1,0:T(8,128)S(1)} %copy.18), custom_call_target="Cholesky" | custom-call | tf_op jit(solution)/shard_map/jit(cholesky)/cholesky | solution.py:10
  153.7 0.8 collective-permute-start.2
  154.6 3.0 %collective-permute-done.2 = f32[32,64]{1,0:T(8,128)S(1)} collective-permute-done((f32[32,64]{1,0:T(8,128)S(1)}, f32[32,64]{1,0:T(8,128)S(1)}, u32[]{:S(2)}, u32[]{:S(2)}) %collective-permute-start.2) | collective-permute-done | bytes 8224 | tf_op jit(solution)/shard_map/ppermute | solution.py:45
  157.5 1.0 collective-permute-start.3
  159.2 3.0 %collective-permute-done.3 = f32[32,64]{1,0:T(8,128)S(1)} collective-permute-done((f32[32,64]{1,0:T(8,128)S(1)}, f32[32,64]{1,0:T(8,128)S(1)}, u32[]{:S(2)}, u32[]{:S(2)}) %collective-permute-start.3) | collective-permute-done | bytes 8224 | tf_op jit(solution)/shard_map/ppermute | solution.py:45
  162.2 3.1 %collective-permute-start.4 = (f32[32,64]{1,0:T(8,128)S(1)}, f32[32,64]{1,0:T(8,128)S(1)}, u32[]{:S(2)}, u32[]{:S(2)}) collective-permute-start(f32[32,64]{1,0:T(8,128)S(1)} %add.64), channel_id=1, source_target_pairs={{0,128},{8,136},{16,144},{24,152},{32,160},{40,168},{48,176},{56,1... | collective-permute-start | bytes 24584 | tf_op jit(solution)/shard_map/ppermute | solution.py:45
  166.0 4.9 %custom-call.24 = f32[1,64,64]{1,2,0:T(8,128)S(1)} custom-call(f32[1,64,64]{2,1,0:T(8,128)S(1)} %fusion.3), custom_call_target="InvertDiagBlocksLowerTriangular" | custom-call | tf_op jit(solution)/shard_map/jit(_cho_solve)/triangular_solve | solution.py:11
  171.6 72.9 %psum.31 = f32[16,64]{1,0:T(8,128)S(1)} all-reduce(f32[16,64]{1,0:T(8,128)S(1)} %multiply_reduce_fusion), channel_id=1, replica_groups=mesh['link'=32,'intv'=8] {'link','intv'}, use_global_device_ids=true, to_apply=%region_11.13 | all-reduce | flops 1024 | bytes 8192 | tf_op jit(solution)/shard_map/psum | solution.py:51
  244.5 24.6 %psum.30 = f32[64,64]{1,0:T(8,128)S(1)} all-reduce(f32[64,64]{1,0:T(8,128)S(1)} %fusion.35), channel_id=1, replica_groups=mesh['link'=32,'intv'=8] {'intv'}, use_global_device_ids=true, to_apply=%region_8.10 | all-reduce | flops 4096 | bytes 32768 | tf_op jit(solution)/shard_map/psum | solution.py:49
  270.5 5.9 %cholesky.81 = f32[64,64]{1,0:T(8,128)S(1)} custom-call(f32[64,64]{1,0:T(8,128)S(1)} %copy.21), custom_call_target="Cholesky" | custom-call | tf_op jit(solution)/shard_map/jit(cholesky)/cholesky | solution.py:10
  277.7 4.9 %custom-call.25 = f32[1,64,64]{1,2,0:T(8,128)S(1)} custom-call(f32[1,64,64]{2,1,0:T(8,128)S(1)} %fusion.4), custom_call_target="InvertDiagBlocksLowerTriangular" | custom-call | tf_op jit(solution)/shard_map/jit(_cho_solve)/triangular_solve | solution.py:11
  282.9 0.8 fusion.5
  (53 shorter events, 7.5 us)
Async XLA Ops:
  7.2 32.7 %copy-start.3 = (f32[16,64]{1,0:T(8,128)S(1)}, f32[16,64]{1,0:T(8,128)}, u32[]{:S(2)}) copy-start(f32[16,64]{1,0:T(8,128)} %param.6) | copy-start | bytes 12292
  7.2 6.5 %copy-start.1 = (f32[32,64]{1,0:T(8,128)S(1)}, f32[32,64]{1,0:T(8,128)}, u32[]{:S(2)}) copy-start(f32[32,64]{1,0:T(8,128)} %param.5) | copy-start | bytes 24580
  7.2 46.4 %reduce-scatter.2.cloned.1.call-start = ((), (), s32[]{:S(2)}) async-start(), calls=%async_computation.1 | async-start | bytes 2359296 | tf_op jit(solution)/shard_map/reduce_scatter | solution.py:30
  13.6 122.4 %all-gather.2.cloned.1.call-start = ((), (), s32[]{:S(2)}) async-start(), calls=%async_computation.2 | async-start | bytes 1179648 | tf_op jit(solution)/shard_map/all_gather | solution.py:38
  55.4 228.4 %copy-start = (f32[64,1024]{1,0:T(8,128)}, f32[64,1024]{1,0:T(8,128)S(1)}, u32[]{:S(2)}) copy-start(f32[64,1024]{1,0:T(8,128)S(1)} %fusion.15) | copy-start | bytes 786436
  142.7 3.8 %collective-permute-start = (f32[32,64]{1,0:T(8,128)S(1)}, f32[32,64]{1,0:T(8,128)S(1)}, u32[]{:S(2)}, u32[]{:S(2)}) collective-permute-start(f32[32,64]{1,0:T(8,128)S(1)} %multiply_reduce_fusion.1), channel_id=1, source_target_pairs={{0,8},{8,0},{16,24},{24,16},{32,40},{40,32},{48,56},{56,48},{64,72... | collective-permute-start | bytes 24584 | tf_op jit(solution)/shard_map/ppermute | solution.py:45
  146.5 7.2 %collective-permute-start.1 = (f32[32,64]{1,0:T(8,128)S(1)}, f32[32,64]{1,0:T(8,128)S(1)}, u32[]{:S(2)}, u32[]{:S(2)}) collective-permute-start(f32[32,64]{1,0:T(8,128)S(1)} %add.61), channel_id=1, source_target_pairs={{0,16},{8,24},{16,0},{24,8},{32,48},{40,56},{48,32},{56,40},{64,80... | collective-permute-start | bytes 24584 | tf_op jit(solution)/shard_map/ppermute | solution.py:45
  153.7 3.8 %collective-permute-start.2 = (f32[32,64]{1,0:T(8,128)S(1)}, f32[32,64]{1,0:T(8,128)S(1)}, u32[]{:S(2)}, u32[]{:S(2)}) collective-permute-start(f32[32,64]{1,0:T(8,128)S(1)} %add.62), channel_id=1, source_target_pairs={{0,32},{8,40},{16,48},{24,56},{32,0},{40,8},{48,16},{56,24},{64,96... | collective-permute-start | bytes 24584 | tf_op jit(solution)/shard_map/ppermute | solution.py:45
  157.5 4.6 %collective-permute-start.3 = (f32[32,64]{1,0:T(8,128)S(1)}, f32[32,64]{1,0:T(8,128)S(1)}, u32[]{:S(2)}, u32[]{:S(2)}) collective-permute-start(f32[32,64]{1,0:T(8,128)S(1)} %add.63), channel_id=1, source_target_pairs={{0,64},{8,72},{16,80},{24,88},{32,96},{40,104},{48,112},{56,120},{... | collective-permute-start | bytes 24584 | tf_op jit(solution)/shard_map/ppermute | solution.py:45
  162.2 8.7 %collective-permute-start.4 = (f32[32,64]{1,0:T(8,128)S(1)}, f32[32,64]{1,0:T(8,128)S(1)}, u32[]{:S(2)}, u32[]{:S(2)}) collective-permute-start(f32[32,64]{1,0:T(8,128)S(1)} %add.64), channel_id=1, source_target_pairs={{0,128},{8,136},{16,144},{24,152},{32,160},{40,168},{48,176},{56,1... | collective-permute-start | bytes 24584 | tf_op jit(solution)/shard_map/ppermute | solution.py:45
  171.3 112.4 %copy-start.2 = (f32[64,32]{0,1:T(8,128)}, f32[64,32]{0,1:T(8,128)S(1)}, u32[]{:S(2)}) copy-start(f32[64,32]{0,1:T(8,128)S(1)} %fusion.10) | copy-start | bytes 24580
Sparse Core Ops, SparseCore 0:
  13.8 38.9 reduce-scatter.1
  56.3 25.9 all-gather.1
